TPU v7x, 256 devices: a whole 4x4x8 slice. The times are simulated.
256 devices in a mesh: tm: 64 (over x, z, core), chan: 4 (over y).
Axes of the slice: x: 4, y: 4, z: 8, core: 2. Of those that a mesh axis runs over, the one named last changes fastest.
Arguments:
- features: bfloat16 [393216, 512], P('tm', 'chan'), may hold values from -6 to 6
- snake_alpha: float32 [512], P('chan'), may hold values from 0.5 to 3
- down_weight: bfloat16 [512, 16, 1024], P(None, None, 'chan'), may hold values from -0.0625 to 0.0625
- grad_out: bfloat16 [49152, 1024], P('tm', 'chan'), may hold values from -6 to 6
Outputs:
- encoded: bfloat16 [49152, 1024], P('tm', 'chan')
- grad_features: bfloat16 [393216, 512], P('tm', 'chan')
- grad_down: bfloat16 [1024, 16, 512], P('tm', None, 'chan')
All inputs are finite; a program needn't handle non-finite values.
Results may differ from a plain program's by a relative error of at most 0.0049.
Values may be sent and summed in bfloat16 or wider, within the bound.
No kernel may reach another device: no remote copies, remote signals or barrier semaphores. Data moves between devices by JAX's collectives and lax.ppermute only.
A program may use at most 128 MiB of HBM per device.

v0:
```python
import math
import jax
import jax.numpy as jnp
from jax import lax
from jax.sharding import PartitionSpec as P

STRIDE = 8


def with_halo(block, sides, width):
    for axis, dim in sides:
        count = lax.axis_size(axis)
        forward = [(i, i + 1) for i in range(count - 1)]
        backward = [(target, source) for source, target in forward]
        low = lax.ppermute(
            lax.slice_in_dim(block, block.shape[dim] - width, None, axis=dim), axis, forward
        )
        high = lax.ppermute(lax.slice_in_dim(block, 0, width, axis=dim), axis, backward)
        block = jnp.concatenate([low, block, high], axis=dim)
    return block


def snake(values, alpha):
    return values + jnp.sin(alpha * values) ** 2 / alpha


def shards(features, snake_alpha, down_weight, grad_out):
    frames = features.shape[0]
    local_chans = features.shape[1]
    blocks_out = frames // STRIDE
    offset = STRIDE // 2
    wide = features.astype(jnp.float32)
    snaked = snake(wide, snake_alpha).astype(jnp.bfloat16)
    padded = with_halo(snaked, (("tm", 0),), offset)
    local_tiled = padded.reshape(blocks_out + 1, STRIDE, local_chans)
    full_cols = lax.all_gather(padded, "chan", axis=1, tiled=True)
    tiled = full_cols.reshape(blocks_out + 1, STRIDE, full_cols.shape[1])
    encoded = (
        jnp.einsum(
            "ujr,rjp->up", tiled[:-1], down_weight[:, :STRIDE], preferred_element_type=jnp.float32
        )
        + jnp.einsum(
            "ujr,rjp->up", tiled[1:], down_weight[:, STRIDE:], preferred_element_type=jnp.float32
        )
    ).astype(jnp.bfloat16)
    grad_pad = with_halo(grad_out, (("tm", 0),), 1)
    grad_full = lax.all_gather(grad_pad, "chan", axis=1, tiled=True)
    spread = jnp.einsum(
        "up,rjp->ujr", grad_pad[1:], down_weight[:, :STRIDE], preferred_element_type=jnp.float32
    ) + jnp.einsum(
        "up,rjp->ujr", grad_pad[:-1], down_weight[:, STRIDE:], preferred_element_type=jnp.float32
    )
    partial_terms = spread.reshape(frames + STRIDE, down_weight.shape[0])[offset : offset + frames]
    grad_snaked = lax.psum_scatter(partial_terms, "chan", scatter_dimension=1, tiled=True)
    grad_features = (grad_snaked * (1.0 + jnp.sin(2.0 * snake_alpha * wide))).astype(jnp.bfloat16)
    grad_inner = grad_full[1:-1]
    scale = 1.0 / math.sqrt(blocks_out * lax.axis_size("tm"))
    lower = jnp.einsum(
        "ujr,up->pjr", local_tiled[:-1], grad_inner, preferred_element_type=jnp.float32
    )
    upper = jnp.einsum(
        "ujr,up->pjr", local_tiled[1:], grad_inner, preferred_element_type=jnp.float32
    )
    summed = lax.psum_scatter(
        jnp.concatenate([lower, upper], axis=1), "tm", scatter_dimension=0, tiled=True
    )
    grad_down = (summed * scale).astype(jnp.bfloat16)
    return (encoded, grad_features, grad_down)


def solution(mesh):
    placed = (P("tm", "chan"), P("chan"), P(None, None, "chan"), P("tm", "chan"))
    return jax.shard_map(
        shards,
        mesh=mesh,
        in_specs=placed,
        out_specs=(P("tm", "chan"), P("tm", "chan"), P("tm", None, "chan")),
        check_vma=False,
    )
```

profile of v0, /device:TPU:8, one launch (start us, length us, event | category | flops | bytes accessed | tf_op | source)
XLA Modules:
  0.0 450.1 jit_solution(14186953188106699410)
XLA Ops:
  7.2 0.7 fusion.51
  7.9 1.7 collective-permute-start.3
  9.7 1.4 collective-permute-start.2
  11.1 2.5 fusion.49
  13.6 1.9 fusion.12
  15.5 0.1 copy-done.2
  15.6 6.7 %add_bitcast_fusion = f32[769,8,512]{2,0,1:T(8,128)} fusion(f32[769,512,8]{1,0,2:T(8,128)S(1)} %fusion.12, bf16[512,8,256]{2,1,0:T(8,128)(2,1)S(1)} %get-tuple-element.11, bf16[1,256]{1,0:T(2,128)(2,1)S(1)} %collective-permute-done.2, bf16[768,256]{1,0:T(8,128)(2,1)S(1)} %copy-done.4), kind=kOutput, calls=%fused_computation | convolution fusion | flops 1616647168 | bytes 27689472 | tf_op jit(solution)/shard_map/up,rjp->ujr/dot_general | solution.py:48
  22.3 16.4 %copy.59 = f32[769,8,512]{2,1,0:T(8,128)} copy(f32[769,8,512]{2,0,1:T(8,128)} %add_bitcast_fusion) | data formatting | bytes 25198592 | tf_op jit(solution)/shard_map/add | solution.py:48
  38.8 10.9 %slice.76 = f32[6144,512]{1,0:T(8,128)} slice(f32[6152,512]{1,0:T(8,128)} %bitcast.31), slice={[4:6148], [0:512]} | slice | bytes 25165824 | tf_op jit(solution)/shard_map/slice | solution.py:53
  49.7 0.0 all-gather.5.cloned.1.call-start
  49.7 0.2 copy.19
  49.9 0.1 copy.18
  50.0 0.1 copy.20
  50.2 1.0 pad_maximum_fusion.3
  51.3 121.0 %reduce-scatter.3.cloned.1.call-done = f32[6144,128]{1,0:T(8,128)} async-done(((f32[6144,512]{1,0:T(8,128)}), f32[6144,128]{1,0:T(8,128)}) %reduce-scatter.3.cloned.1.call-update) | async-done | bytes 3145744 | tf_op jit(solution)/shard_map/reduce_scatter | solution.py:54
  172.3 23.1 %fusion.11 = (bf16[6144,128]{1,0:T(8,128)(2,1)}, bf16[6144,128]{1,0:T(8,128)(2,1)S(1)}) fusion(f32[6144,128]{1,0:T(8,128)} %reduce-scatter.3.cloned.1.call-done, bf16[6144,128]{1,0:T(8,128)(2,1)S(1)} %copy-done.5, f32[128]{0:T(128)S(1)} %broadcast_multiply_fusion, f32[128]{0:T(128)S(1)} %copy-done.6), kind=kLoop, calls=%fused_computation.19 | loop fusion | flops 7864320 | bytes 7865344 | tf_op jit(solution)/shard_map/convert_element_type | solution.py:55
  195.3 1.8 collective-permute-start
  197.1 1.3 collective-permute-start.1
  198.4 3.0 collective-permute-done.1
  201.4 8.7 %concatenate.21 = bf16[6152,128]{1,0:T(8,128)(2,1)} concatenate(bf16[4,128]{1,0:T(4,128)(2,1)S(1)} %collective-permute-done, bf16[6144,128]{1,0:T(8,128)(2,1)S(1)} %get-tuple-element.16, bf16[4,128]{1,0:T(4,128)(2,1)S(1)} %collective-permute-done.1), dimensions={0} | concatenate | bytes 3149824 | tf_op jit(solution)/shard_map/concatenate | solution.py:19
  210.1 0.0 reduce-scatter.5.cloned.1.call-start
  210.2 1.6 fusion.18
  211.8 3.9 fusion.21
  215.7 1.8 fusion.19
  217.6 3.8 pad_maximum_fusion
  221.4 63.4 %all-gather.3.cloned.1.call-done = bf16[6152,512]{1,0:T(8,128)(2,1)} async-done(((bf16[6152,128]{1,0:T(8,128)(2,1)}), bf16[6152,512]{1,0:T(8,128)(2,1)}) %all-gather.3.cloned.1.call-update) | async-done | bytes 6299664 | tf_op jit(solution)/shard_map/all_gather | solution.py:36
  284.8 5.3 %slice_bitcast_fusion.1 = (bf16[768,8,512]{2,1,0:T(8,128)(2,1)S(1)}, bf16[768,8,512]{2,1,0:T(8,128)(2,1)S(1)}) fusion(bf16[6152,512]{1,0:T(8,128)(2,1)} %all-gather.3.cloned.1.call-done), kind=kLoop, calls=%fused_computation.4 | loop fusion | bytes 25165824 | tf_op jit(solution)/shard_map/slice | solution.py:40
  290.1 3.9 fusion.28
  294.1 4.7 %fusion.38 = bf16[768,256]{1,0:T(8,128)(2,1)} fusion(f32[768,256]{1,0:T(8,128)S(1)} %fusion.28, bf16[512,8,256]{2,1,0:T(8,128)(2,1)S(1)} %copy-done.3, bf16[768,8,512]{2,1,0:T(8,128)(2,1)S(1)} %get-tuple-element.9), kind=kOutput, calls=%fused_computation.37 | convolution fusion | flops 1611005952 | bytes 9568256 | tf_op jit(solution)/shard_map/ujr,rjp->up/dot_general | solution.py:39
  298.8 143.3 %reduce-scatter.5.cloned.1.call-done = f32[16,16,128]{2,0,1:T(8,128)} async-done(((f32[1024,16,128]{2,0,1:T(8,128)}), f32[16,16,128]{2,0,1:T(8,128)}) %reduce-scatter.5.cloned.1.call-update) | async-done | bytes 131088 | tf_op jit(solution)/shard_map/reduce_scatter | solution.py:64
  442.0 0.9 multiply_convert_fusion
  443.0 0.6 copy.23
  (27 shorter events, 0.2 us)
Async XLA Ops:
  7.2 165.1 %reduce-scatter.3.cloned.1.call-start = ((), (), s32[]{:S(2)}) async-start(), calls=%async_computation.3 | async-start | bytes 15728640 | tf_op jit(solution)/shard_map/reduce_scatter | solution.py:54
  7.9 5.7 %collective-permute-start.3 = (bf16[1,256]{1,0:T(2,128)(2,1)S(1)}, bf16[1,256]{1,0:T(2,128)(2,1)S(1)}, u32[]{:S(2)}, u32[]{:S(2)}) collective-permute-start(bf16[1,256]{1,0:T(2,128)(2,1)S(1)} %get-tuple-element.20), channel_id=1, source_target_pairs={{0,4},{4,8},{8,12},{12,16},{16,20},{20,24},{24,28},{28,32},{32,36}... | collective-permute-start | bytes 1544 | tf_op jit(solution)/shard_map/ppermute | solution.py:15
  9.7 4.0 copy-start.4
  9.7 5.9 %collective-permute-start.2 = (bf16[1,256]{1,0:T(2,128)(2,1)S(1)}, bf16[1,256]{1,0:T(2,128)(2,1)S(1)}, u32[]{:S(2)}, u32[]{:S(2)}) collective-permute-start(bf16[1,256]{1,0:T(2,128)(2,1)S(1)} %get-tuple-element.19), channel_id=1, source_target_pairs={{4,0},{8,4},{12,8},{16,12},{20,16},{24,20},{28,24},{32,28},{36,32}... | collective-permute-start | bytes 1544 | tf_op jit(solution)/shard_map/ppermute | solution.py:18
  13.6 1.9 copy-start
  13.6 2.0 copy-start.2
  49.6 1.6 copy-start.6
  49.7 122.6 %copy-start.5 = (bf16[6144,128]{1,0:T(8,128)(2,1)S(1)}, bf16[6144,128]{1,0:T(8,128)(2,1)}, u32[]{:S(2)}) copy-start(bf16[6144,128]{1,0:T(8,128)(2,1)} %param.4) | copy-start | bytes 4718596
  49.7 162.1 %all-gather.5.cloned.1.call-start = ((), (), s32[]{:S(2)}) async-start(), calls=%async_computation.4 | async-start | bytes 2293760 | tf_op jit(solution)/shard_map/all_gather | solution.py:47
  51.2 233.6 %all-gather.3.cloned.1.call-start = ((), (), s32[]{:S(2)}) async-start(), calls=%async_computation.2 | async-start | bytes 7874560 | tf_op jit(solution)/shard_map/all_gather | solution.py:36
  195.3 3.1 collective-permute-start
  197.1 4.3 collective-permute-start.1
  210.1 231.9 %reduce-scatter.5.cloned.1.call-start = ((), (), s32[]{:S(2)}) async-start(), calls=%async_computation.5 | async-start | bytes 8519680 | tf_op jit(solution)/shard_map/reduce_scatter | solution.py:64
  211.8 3.9 copy-start.7
  221.4 68.7 %copy-start.1 = (bf16[512,8,256]{2,1,0:T(8,128)(2,1)S(1)}, bf16[512,8,256]{2,1,0:T(8,128)(2,1)}, u32[]{:S(2)}) copy-start(bf16[512,8,256]{2,1,0:T(8,128)(2,1)} %copy-done) | copy-start | bytes 6291460
  290.1 3.9 copy-start.3
Sparse Core Ops, SparseCore 0:
  49.8 122.4 reduce-scatter.2
  174.1 31.2 all-gather.4
  210.3 74.5 all-gather.2
  288.9 153.1 reduce-scatter.4
where the time goes:
time: 451 us; the launch traced here: 450 us
  waiting for transfers between devices  331 us (73%)
  local copies, waits for them, and re-layouts  45.7 us (10%)
  other arithmetic  30.4 us (7%)
  matrix products  23 us (5%)
  between operations  14 us (3%)
  starting transfers between devices  6.38 us (1%)
    reduce_scatter x1, waiting for transfers between devices, shards(): lax.psum_scatter(jnp.concatenate([lower, upper], axis=1), 'tm', scatter_d...  143 us
    reduce_scatter x1, waiting for transfers between devices, shards(): lax.psum_scatter(partial_terms, 'chan', scatter_dimension=1, tiled=True)  121 us
    all_gather x1, waiting for transfers between devices, shards(): full_cols = lax.all_gather(padded, 'chan', axis=1, tiled=True)  63.4 us
    convert_element_type x1, other arithmetic, shards(): (grad_snaked * (1.0 + jnp.sin(2.0 * snake_alpha * wide))).astype(jnp.bflo...  23.1 us
    add x1, local copies, waits for them, and re-layouts, shards(): jnp.einsum('up,rjp->ujr', grad_pad[1:], down_weight[:, :STRIDE], preferre...  16.4 us
    slice x1, local copies, waits for them, and re-layouts, shards(): spread.reshape(frames + STRIDE, down_weight.shape[0])  10.9 us
  transfers between devices with their start and end apart: 8, of which 4 were waited for; matrix products, arithmetic and copies ran while one was open for 14% of the time, Pallas kernels for 0%

commit v1 on v0

--- a/solution.py
+++ b/solution.py
@@ -33,7 +33,16 @@
     snaked = snake(wide, snake_alpha).astype(jnp.bfloat16)
     padded = with_halo(snaked, (("tm", 0),), offset)
     local_tiled = padded.reshape(blocks_out + 1, STRIDE, local_chans)
-    full_cols = lax.all_gather(padded, "chan", axis=1, tiled=True)
+    ways = lax.axis_size("chan")
+    up = [(d, (d + 1) % ways) for d in range(ways)]
+    down = [(d, (d - 1) % ways) for d in range(ways)]
+    earlier, later = ([padded], [padded])
+    for _ in range(ways // 2):
+        earlier.append(lax.ppermute(earlier[-1], "chan", up))
+    for _ in range((ways - 1) // 2):
+        later.append(lax.ppermute(later[-1], "chan", down))
+    line = jnp.concatenate([*earlier[::-1], *later[1:]], axis=1)
+    full_cols = jnp.roll(line, (lax.axis_index("chan") - ways // 2) * padded.shape[1], axis=1)
     tiled = full_cols.reshape(blocks_out + 1, STRIDE, full_cols.shape[1])
     encoded = (
         jnp.einsum(

time: 451 us -> 375 us (0.83)
  waiting for transfers between devices: 331 us -> 233 us
  local copies, waits for them, and re-layouts: 45.7 us -> 58.7 us
  starting transfers between devices: 6.38 us -> 13 us
    reduce_scatter x1, waiting for transfers between devices: 143 us -> 41.3 us  [shards(): lax.psum_scatter(jnp.concatenate([lower, upper], axis=1), 'tm', scatter_d...]
    ppermute x0 -> x3, waiting for transfers between devices: none -> 68.6 us  [the longest x2 68.6 us: shards(): earlier.append(lax.ppermute(earlier[-1], 'chan', up))]
    all_gather x1 -> x0, waiting for transfers between devices: 63.4 us -> none  [shards(): full_cols = lax.all_gather(padded, 'chan', axis=1, tiled=True)]
    unnamed x18 -> x25, local copies, waits for them, and re-layouts: 0.92 us -> 13.5 us
    concatenate x1, local copies, waits for them, and re-layouts: 8.69 us -> 2.61 us  [with_halo(): block = jnp.concatenate([low, block, high], axis=dim)]
    slice x1, local copies, waits for them, and re-layouts: 5.28 us -> 10.4 us  [shards(): tiled[:-1]]
  transfers between devices with their start and end apart: 8 -> 10, of which waited for: 4 -> 6; matrix products, arithmetic and copies ran while one was open for 14% -> 18% of each run, Pallas kernels for 0% -> 0%
where the time goes in v1:
time: 375 us
  waiting for transfers between devices  233 us (62%)
  local copies, waits for them, and re-layouts  58.7 us (16%)
  other arithmetic  30.4 us (8%)
  matrix products  26 us (7%)
  between operations  13.9 us (4%)
  starting transfers between devices  13 us (3%)
    reduce_scatter x1, waiting for transfers between devices, shards(): lax.psum_scatter(partial_terms, 'chan', scatter_dimension=1, tiled=True)  119 us
    ppermute x2, waiting for transfers between devices, shards(): earlier.append(lax.ppermute(earlier[-1], 'chan', up))  68.6 us
    reduce_scatter x1, waiting for transfers between devices, shards(): lax.psum_scatter(jnp.concatenate([lower, upper], axis=1), 'tm', scatter_d...  41.3 us
    convert_element_type x1, other arithmetic, shards(): (grad_snaked * (1.0 + jnp.sin(2.0 * snake_alpha * wide))).astype(jnp.bflo...  23.1 us
    add x1, local copies, waits for them, and re-layouts, shards(): jnp.einsum('up,rjp->ujr', grad_pad[1:], down_weight[:, :STRIDE], preferre...  16.4 us
    unnamed x25, local copies, waits for them, and re-layouts  13.5 us
    slice x1, local copies, waits for them, and re-layouts, shards(): spread.reshape(frames + STRIDE, down_weight.shape[0])  10.9 us
    slice x1, local copies, waits for them, and re-layouts, shards(): tiled[:-1]  10.4 us
  transfers between devices with their start and end apart: 10, of which 6 were waited for; matrix products, arithmetic and copies ran while one was open for 18% of the time, Pallas kernels for 0%

profile of v1, /device:TPU:8, one launch (start us, length us, event | category | flops | bytes accessed | tf_op | source)
XLA Modules:
  0.0 374.7 jit_solution(9978480500615866175)
XLA Ops:
  7.9 1.3 collective-permute-start.5
  9.2 3.2 collective-permute-start.6
  12.4 2.5 fusion.49
  14.9 1.9 fusion.12
  16.9 6.7 %add_bitcast_fusion = f32[769,8,512]{2,0,1:T(8,128)} fusion(f32[769,512,8]{1,0,2:T(8,128)S(1)} %fusion.12, bf16[512,8,256]{2,1,0:T(8,128)(2,1)S(1)} %get-tuple-element.11, bf16[1,256]{1,0:T(2,128)(2,1)S(1)} %collective-permute-done.5, bf16[768,256]{1,0:T(8,128)(2,1)S(1)} %copy-done.5), kind=kOutput, calls=%fused_computation | convolution fusion | flops 1616647168 | bytes 27689472 | tf_op jit(solution)/shard_map/up,rjp->ujr/dot_general | solution.py:57
  23.6 16.4 %copy.59 = f32[769,8,512]{2,1,0:T(8,128)} copy(f32[769,8,512]{2,0,1:T(8,128)} %add_bitcast_fusion) | data formatting | bytes 25198592 | tf_op jit(solution)/shard_map/add | solution.py:57
  40.1 10.9 %slice.74 = f32[6144,512]{1,0:T(8,128)} slice(f32[6152,512]{1,0:T(8,128)} %bitcast.31), slice={[4:6148], [0:512]} | slice | bytes 25165824 | tf_op jit(solution)/shard_map/slice | solution.py:62
  52.6 118.7 %reduce-scatter.3.cloned.1.call-done = f32[6144,128]{1,0:T(8,128)} async-done(((f32[6144,512]{1,0:T(8,128)}), f32[6144,128]{1,0:T(8,128)}) %reduce-scatter.3.cloned.1.call-update) | async-done | bytes 3145744 | tf_op jit(solution)/shard_map/reduce_scatter | solution.py:63
  171.3 23.1 %fusion.11 = (bf16[6144,128]{1,0:T(8,128)(2,1)}, bf16[6144,128]{1,0:T(8,128)(2,1)S(1)}) fusion(f32[6144,128]{1,0:T(8,128)} %reduce-scatter.3.cloned.1.call-done, bf16[6144,128]{1,0:T(8,128)(2,1)} %param.4, f32[128]{0:T(128)S(1)} %broadcast_multiply_fusion, f32[128]{0:T(128)S(1)} %copy-done.6), kind=kLoop, calls=%fused_computation.19 | loop fusion | flops 7864320 | bytes 7865344 | tf_op jit(solution)/shard_map/convert_element_type | solution.py:64
  194.5 1.3 collective-permute-start.1
  195.8 3.0 collective-permute-start
  199.6 1.6 fusion.18
  201.2 3.2 all-gather.2.cloned.1.call-done
  204.4 3.9 %fusion.21 = f32[1024,8,128]{2,0,1:T(8,128)S(1)} fusion(bf16[768,8,128]{2,1,0:T(8,128)(2,1)} %get-tuple-element.13, bf16[770,1024]{0,1:T(8,128)(2,1)} %all-gather.2.cloned.1.call-done), kind=kOutput, calls=%fused_computation.32 | convolution fusion | flops 1610612736 | bytes 7340032 | tf_op jit(solution)/shard_map/ujr,up->pjr/dot_general | solution.py:67
  208.3 1.8 fusion.19
  210.2 3.8 %pad_maximum_fusion = f32[1024,16,128]{2,0,1:T(8,128)} fusion(f32[1024,8,128]{2,0,1:T(8,128)S(1)} %fusion.19, f32[1024,8,128]{2,0,1:T(8,128)S(1)} %fusion.21), kind=kLoop, calls=%fused_computation.2 | loop fusion | flops 2097152 | bytes 16777216 | tf_op jit(solution)/shard_map/concatenate | solution.py:74
  214.0 2.6 concatenate.27
  217.9 35.0 %collective-permute-done.2 = bf16[6152,128]{1,0:T(8,128)(2,1)S(1)} collective-permute-done((bf16[6152,128]{1,0:T(8,128)(2,1)S(1)}, bf16[6152,128]{1,0:T(8,128)(2,1)S(1)}, u32[]{:S(2)}, u32[]{:S(2)}) %collective-permute-start.2) | collective-permute-done | bytes 1574944 | tf_op jit(solution)/shard_map/ppermute | solution.py:41
  254.1 1.6 collective-permute-start.4
  255.7 33.7 %collective-permute-done.3 = bf16[6152,128]{1,0:T(8,128)(2,1)} collective-permute-done((bf16[6152,128]{1,0:T(8,128)(2,1)S(1)}, bf16[6152,128]{1,0:T(8,128)(2,1)}, u32[]{:S(2)}, u32[]{:S(2)}) %collective-permute-start.3) | collective-permute-done | bytes 1574944 | tf_op jit(solution)/shard_map/ppermute | solution.py:41
  289.3 2.8 constant_dynamic-update-slice_fusion.7
  292.1 1.4 constant_dynamic-update-slice_fusion.6
  293.6 1.4 constant_dynamic-update-slice_fusion.5
  295.0 1.4 constant_dynamic-update-slice_fusion.4
  296.4 2.8 constant_dynamic-update-slice_fusion.3
  299.2 1.4 constant_dynamic-update-slice_fusion.2
  300.5 1.4 constant_dynamic-update-slice_fusion.1
  301.9 1.3 constant_dynamic-update-slice_fusion
  303.3 10.4 %dynamic-slice_bitcast_fusion.1 = (bf16[768,8,512]{2,1,0:T(8,128)(2,1)}, bf16[768,8,512]{2,1,0:T(8,128)(2,1)}) fusion(bf16[6152,1024]{1,0:T(8,128)(2,1)} %constant_dynamic-update-slice_fusion, s32[]{:T(128)S(6)} %select_n.14, s32[]{:T(128)S(6)} %add.41), kind=kLoop, calls=%fused_computation.4 | loop fusion | bytes 25165832 | tf_op jit(solution)/shard_map/slice | solution.py:49
  313.7 6.9 %fusion.28 = f32[768,256]{1,0:T(8,128)S(1)} fusion(bf16[512,8,256]{2,1,0:T(8,128)(2,1)S(1)} %copy-done.1, bf16[768,8,512]{2,1,0:T(8,128)(2,1)} %get-tuple-element.10), kind=kOutput, calls=%fused_computation.35 | convolution fusion | flops 1610612736 | bytes 9175040 | tf_op jit(solution)/shard_map/ujr,rjp->up/dot_general | solution.py:51
  320.6 4.7 %fusion.38 = bf16[768,256]{1,0:T(8,128)(2,1)} fusion(f32[768,256]{1,0:T(8,128)S(1)} %fusion.28, bf16[512,8,256]{2,1,0:T(8,128)(2,1)S(1)} %copy-done.3, bf16[768,8,512]{2,1,0:T(8,128)(2,1)S(1)} %copy-done.4), kind=kOutput, calls=%fused_computation.37 | convolution fusion | flops 1611005952 | bytes 9568256 | tf_op jit(solution)/shard_map/ujr,rjp->up/dot_general | solution.py:48
  325.3 41.3 %reduce-scatter.5.cloned.1.call-done = f32[16,16,128]{2,0,1:T(8,128)} async-done(((f32[1024,16,128]{2,0,1:T(8,128)}), f32[16,16,128]{2,0,1:T(8,128)}) %reduce-scatter.5.cloned.1.call-update) | async-done | bytes 131088 | tf_op jit(solution)/shard_map/reduce_scatter | solution.py:73
  (38 shorter events, 7.3 us)
Async XLA Ops:
  7.2 164.2 %reduce-scatter.3.cloned.1.call-start = ((), (), s32[]{:S(2)}) async-start(), calls=%async_computation.2 | async-start | bytes 15728640 | tf_op jit(solution)/shard_map/reduce_scatter | solution.py:63
  7.9 8.9 %collective-permute-start.5 = (bf16[1,256]{1,0:T(2,128)(2,1)S(1)}, bf16[1,256]{1,0:T(2,128)(2,1)S(1)}, u32[]{:S(2)}, u32[]{:S(2)}) collective-permute-start(bf16[1,256]{1,0:T(2,128)(2,1)S(1)} %get-tuple-element.19), channel_id=1, source_target_pairs={{4,0},{8,4},{12,8},{16,12},{20,16},{24,20},{28,24},{32,28},{36,32}... | collective-permute-start | bytes 1544 | tf_op jit(solution)/shard_map/ppermute | solution.py:18
  9.2 5.7 %copy-start.5 = (bf16[768,256]{1,0:T(8,128)(2,1)S(1)}, bf16[768,256]{1,0:T(8,128)(2,1)}, u32[]{:S(2)}) copy-start(bf16[768,256]{1,0:T(8,128)(2,1)} %param.7) | copy-start | bytes 1179652
  9.2 5.7 %collective-permute-start.6 = (bf16[1,256]{1,0:T(2,128)(2,1)S(1)}, bf16[1,256]{1,0:T(2,128)(2,1)S(1)}, u32[]{:S(2)}, u32[]{:S(2)}) collective-permute-start(bf16[1,256]{1,0:T(2,128)(2,1)S(1)} %get-tuple-element.20), channel_id=1, source_target_pairs={{0,4},{4,8},{8,12},{12,16},{16,20},{20,24},{24,28},{28,32},{32,36}... | collective-permute-start | bytes 1544 | tf_op jit(solution)/shard_map/ppermute | solution.py:15
  14.9 1.9 copy-start
  14.9 2.0 copy-start.2
  50.9 1.6 copy-start.6
  51.0 153.4 %all-gather.2.cloned.1.call-start = ((), (), s32[]{:S(2)}) async-start(), calls=%async_computation.3 | async-start | bytes 2293760 | tf_op jit(solution)/shard_map/all_gather | solution.py:56
  52.5 314.0 %reduce-scatter.5.cloned.1.call-start = ((), (), s32[]{:S(2)}) async-start(), calls=%async_computation.4 | async-start | bytes 8519680 | tf_op jit(solution)/shard_map/reduce_scatter | solution.py:73
  194.5 4.3 %collective-permute-start.1 = (bf16[4,128]{1,0:T(4,128)(2,1)S(1)}, bf16[4,128]{1,0:T(4,128)(2,1)S(1)}, u32[]{:S(2)}, u32[]{:S(2)}) collective-permute-start(bf16[4,128]{1,0:T(4,128)(2,1)S(1)} %get-tuple-element.17), channel_id=1, source_target_pairs={{4,0},{8,4},{12,8},{16,12},{20,16},{24,20},{28,24},{32,28},{36,32}... | collective-permute-start | bytes 3080 | tf_op jit(solution)/shard_map/ppermute | solution.py:18
  195.8 3.8 %collective-permute-start = (bf16[4,128]{1,0:T(4,128)(2,1)S(1)}, bf16[4,128]{1,0:T(4,128)(2,1)S(1)}, u32[]{:S(2)}, u32[]{:S(2)}) collective-permute-start(bf16[4,128]{1,0:T(4,128)(2,1)S(1)} %get-tuple-element.18), channel_id=1, source_target_pairs={{0,4},{4,8},{8,12},{12,16},{16,20},{20,24},{24,28},{28,32},{32,36}... | collective-permute-start | bytes 3080 | tf_op jit(solution)/shard_map/ppermute | solution.py:15
  204.4 3.9 %copy-start.7 = (bf16[770,1024]{0,1:T(8,128)(2,1)S(1)}, bf16[770,1024]{0,1:T(8,128)(2,1)}, u32[]{:S(2)}) copy-start(bf16[770,1024]{0,1:T(8,128)(2,1)} %all-gather.2.cloned.1.call-done) | copy-start | bytes 4730884
  216.6 36.2 %collective-permute-start.2 = (bf16[6152,128]{1,0:T(8,128)(2,1)S(1)}, bf16[6152,128]{1,0:T(8,128)(2,1)S(1)}, u32[]{:S(2)}, u32[]{:S(2)}) collective-permute-start(bf16[6152,128]{1,0:T(8,128)(2,1)S(1)} %concatenate.27), channel_id=1, source_target_pairs={{0,1},{1,2},{2,3},{3,0},{4,5},{5,6},{6,7},{7,4},{8,9},{9,10},{10,1... | collective-permute-start | bytes 4724744 | tf_op jit(solution)/shard_map/ppermute | solution.py:41
  252.8 36.5 %collective-permute-start.3 = (bf16[6152,128]{1,0:T(8,128)(2,1)S(1)}, bf16[6152,128]{1,0:T(8,128)(2,1)}, u32[]{:S(2)}, u32[]{:S(2)}) collective-permute-start(bf16[6152,128]{1,0:T(8,128)(2,1)S(1)} %collective-permute-done.2), channel_id=1, source_target_pairs={{0,1},{1,2},{2,3},{3,0},{4,5},{5,6},{6,7},{7,4},{8,9},{9,10},{10,1... | collective-permute-start | bytes 4724744 | tf_op jit(solution)/shard_map/ppermute | solution.py:41
  254.1 40.9 %collective-permute-start.4 = (bf16[6152,128]{1,0:T(8,128)(2,1)S(1)}, bf16[6152,128]{1,0:T(8,128)(2,1)S(1)}, u32[]{:S(2)}, u32[]{:S(2)}) collective-permute-start(bf16[6152,128]{1,0:T(8,128)(2,1)S(1)} %concatenate.27), channel_id=1, source_target_pairs={{0,3},{1,0},{2,1},{3,2},{4,7},{5,4},{6,5},{7,6},{8,11},{9,8},{10,9... | collective-permute-start | bytes 4724744 | tf_op jit(solution)/shard_map/ppermute | solution.py:43
  303.3 10.4 %copy-start.1 = (bf16[512,8,256]{2,1,0:T(8,128)(2,1)S(1)}, bf16[512,8,256]{2,1,0:T(8,128)(2,1)}, u32[]{:S(2)}) copy-start(bf16[512,8,256]{2,1,0:T(8,128)(2,1)} %copy-done) | copy-start | bytes 6291460
  313.7 6.9 %copy-start.3 = (bf16[512,8,256]{2,1,0:T(8,128)(2,1)S(1)}, bf16[512,8,256]{2,1,0:T(8,128)(2,1)}, u32[]{:S(2)}) copy-start(bf16[512,8,256]{2,1,0:T(8,128)(2,1)} %copy-done.2) | copy-start | bytes 6291460
  313.7 6.9 %copy-start.4 = (bf16[768,8,512]{2,1,0:T(8,128)(2,1)S(1)}, bf16[768,8,512]{2,1,0:T(8,128)(2,1)}, u32[]{:S(2)}) copy-start(bf16[768,8,512]{2,1,0:T(8,128)(2,1)} %get-tuple-element.9) | copy-start | bytes 18874372
Sparse Core Ops, SparseCore 0:
  51.1 120.1 reduce-scatter.2
  173.1 31.2 all-gather.1
  214.1 152.4 reduce-scatter.4
